TPU v7x, 256 devices: a whole 4x4x8 slice. The times are simulated.
256 devices in a mesh: dp: 16 (over z, core), expert: 16 (over x, y).
Axes of the slice: x: 4, y: 4, z: 8, core: 2. Of those that a mesh axis runs over, the one named last changes fastest.
Arguments:
- history: bfloat16 [512, 1024, 2048], P(('dp', 'expert')), may hold values from -6 to 6
- lengths: int32 [512], P(('dp', 'expert')), may hold values from 64 to 1024, as said below
- user_query: bfloat16 [512, 2048], P(('dp', 'expert')), may hold values from -1000 to 1000
- pos_item: bfloat16 [512, 2048], P(('dp', 'expert')), may hold values from -6 to 6
- neg_index: int32 [512, 63], P(('dp', 'expert')), may hold values from 0 to 511
- routes: int32 [32768, 2], P(('dp', 'expert')), may hold values from 0 to 15, all different within a row; in each aligned block of 128 rows (0 to 127, 128 to 255, ...) at most 32 rows name the same one
- w_router: bfloat16 [2048, 16], replicated, may hold values from -0.125 to 0.125
- w_gate: bfloat16 [16, 2048, 768], P('expert', 'dp'), may hold values from -0.125 to 0.125
- w_up: bfloat16 [16, 2048, 768], P('expert', 'dp'), may hold values from -0.125 to 0.125
- w_down: bfloat16 [16, 768, 2048], P('expert', None, 'dp'), may hold values from -0.21875 to 0.21875
- out_gain: float32 [2048], replicated, may hold values from 0.25 to 1.75
Outputs:
- losses: float32 [512], P(('dp', 'expert'))
- grad_gate: float32 [16, 2048, 768], P('expert', 'dp')
- grad_up: float32 [16, 2048, 768], P('expert', 'dp')
- grad_down: float32 [16, 768, 2048], P('expert', None, 'dp')
- grad_router: float32 [2048, 16], replicated
Inputs may be any that keep to these rules, and one draw needn't show every extreme that they name: `lengths`: every device's block of 2 users holds one user with all 1024 events. `neg_index`: indices of users anywhere in the batch. `routes`: each row names two different experts; among the rows of one device no expert is named more than 32 times, a bound that some block reaches.
All inputs are finite; a program needn't handle non-finite values.
Results may differ from a plain program's by a relative error of at most 0.017.
Values may be sent and summed in bfloat16 or wider, within the bound.
A program may use at most 128 MiB of HBM per device.

v0:
```python
import math
import jax
import jax.numpy as jnp
from jax import lax
from jax.sharding import Mesh
from jax.sharding import PartitionSpec as P

D = 2048
HEADS = 16
HEAD = 128
FF = 768
CANDS = 64
EXPERT = ("expert_0", "expert_1")
DP = ("dp_0", "dp_1")
DP_EXPERT = ("dp_0", "dp_1", "expert_0", "expert_1")
norm_eps = 1e-06
loss_scale = 1024.0


def sent_together(arrays, axis, dim, along):
    widths = [a.shape[along] for a in arrays]
    both = jnp.concatenate(arrays, axis=along)
    result = lax.all_gather(both, axis, axis=dim, tiled=True)
    return tuple(jnp.split(result, [sum(widths[:k]) for k in range(1, len(widths))], axis=along))


def whole_of(x, axes, dim):
    result = x
    for number in range(len(axes) - 1, -1, -1):
        result = lax.all_gather(result, axes[number], axis=dim, tiled=True)
    return result


def over_axes_2(x, axes):
    for axis in axes:
        x = lax.psum(x, axis)
    return x


def silu_pair(pre_act):
    sigma_val = jax.nn.sigmoid(pre_act)
    return (pre_act * sigma_val, sigma_val * (1.0 + pre_act * (1.0 - sigma_val)))


def rms_round(values):
    scale_inv = lax.rsqrt(jnp.mean(values * values, axis=-1, keepdims=True) + norm_eps)
    return (values * scale_inv).astype(jnp.bfloat16)


def local(
    history,
    lengths,
    user_query,
    pos_item,
    neg_index,
    routes,
    w_router,
    w_gate,
    w_up,
    w_down,
    out_gain,
):
    user_count = history.shape[0]
    hist_len = history.shape[1]
    model_width = history.shape[2]
    experts = w_router.shape[1]
    expert_devs = lax.axis_size(EXPERT)
    capacity = 4 * user_count * CANDS // experts
    slot_count = expert_devs * capacity
    row_total = user_count * CANDS
    query_heads = user_query.reshape(user_count, HEADS, HEAD)
    key_heads = history.reshape(user_count, hist_len, HEADS, HEAD)
    scores = jnp.einsum(
        "uhd,uthd->uht", query_heads, key_heads, preferred_element_type=jnp.float32
    ) / math.sqrt(HEAD)
    live_mask = jnp.arange(hist_len, dtype=jnp.int32)[None, None, :] < lengths[:, None, None]
    scores = jnp.where(live_mask, scores, -1e30)
    top_val = jnp.max(scores, axis=-1, keepdims=True)
    weights = jnp.where(live_mask, jnp.exp(scores - top_val), 0.0)
    attn_probs = (weights / jnp.sum(weights, axis=-1, keepdims=True)).astype(jnp.bfloat16)
    context = jnp.einsum(
        "uht,uthd->uhd", attn_probs, key_heads, preferred_element_type=jnp.float32
    ).reshape(user_count, model_width)
    all_items = lax.all_gather(pos_item, DP_EXPERT, axis=0, tiled=True)
    candidates = jnp.concatenate([pos_item[:, None, :], all_items[neg_index]], axis=1)
    x_sum = candidates.astype(jnp.float32) + context[:, None, :]
    normed = rms_round(x_sum).reshape(row_total, model_width)
    logits = jnp.dot(normed, w_router, preferred_element_type=jnp.float32)
    affinity = jax.nn.sigmoid(jnp.take_along_axis(logits, routes, axis=1))
    aff_total = jnp.sum(affinity, axis=1, keepdims=True)
    mix = affinity / aff_total
    flat_routes = routes.reshape(-1)
    one_hot = (flat_routes[:, None] == jnp.arange(experts, dtype=jnp.int32)[None, :]).astype(
        jnp.int32
    )
    slot_rank = jnp.sum(jnp.cumsum(one_hot, axis=0) * one_hot, axis=1) - 1
    slot_dest = flat_routes * capacity + slot_rank
    user_base = (lax.axis_index(DP) * expert_devs + lax.axis_index(EXPERT)) * user_count
    own_users = user_base + jnp.arange(user_count, dtype=jnp.int32)
    item_ids = jnp.concatenate([own_users[:, None], neg_index], axis=1).reshape(-1)
    user_ids = (own_users[:, None] + jnp.zeros((user_count, CANDS), jnp.int32)).reshape(-1)
    item_send = (
        jnp.zeros((experts * capacity,), jnp.int32).at[slot_dest].set(jnp.repeat(item_ids, 2))
    )
    user_send = (
        jnp.full((experts * capacity,), -1, jnp.int32).at[slot_dest].set(jnp.repeat(user_ids, 2))
    )
    item_got, user_got = (
        lax.all_to_all(
            item_send.reshape(experts, capacity), EXPERT, split_axis=0, concat_axis=0, tiled=True
        ),
        lax.all_to_all(
            user_send.reshape(experts, capacity), EXPERT, split_axis=0, concat_axis=0, tiled=True
        ),
    )
    group_ctx = lax.all_gather(context, EXPERT, axis=0, tiled=True)
    user_flat = user_got.reshape(-1)
    live_slot = (user_flat >= 0)[:, None]
    local_user = jnp.maximum(user_flat - lax.axis_index(DP) * expert_devs * user_count, 0)
    rebuilt = all_items[item_got.reshape(-1)].astype(jnp.float32) + group_ctx[local_user]
    rows_in = jnp.where(live_slot, rms_round(rebuilt), jnp.zeros((), jnp.bfloat16))
    pieces = sent_together((w_gate[0], w_up[0]), DP, 0, 1)
    columns = rows_in
    gate_pre = jnp.dot(columns, pieces[0], preferred_element_type=jnp.float32)
    up_pre = jnp.dot(columns, pieces[1], preferred_element_type=jnp.float32)
    silu_val, silu_grad = silu_pair(gate_pre)
    hidden = (silu_val * up_pre).astype(jnp.bfloat16)
    expert_out = jnp.dot(
        hidden, whole_of(w_down[0], DP, 1), preferred_element_type=jnp.float32
    ).astype(jnp.bfloat16)
    returned = lax.all_to_all(
        expert_out.reshape(expert_devs, capacity, model_width),
        EXPERT,
        split_axis=0,
        concat_axis=0,
        tiled=True,
    )
    mixed_in = returned.reshape(experts * capacity, model_width)[slot_dest].reshape(
        row_total, 2, model_width
    )
    moe_sum = mix[:, 0:1] * mixed_in[:, 0].astype(jnp.float32) + mix[:, 1:2] * mixed_in[
        :, 1
    ].astype(jnp.float32)
    h_rows = (x_sum.reshape(row_total, model_width) + moe_sum).reshape(
        user_count, CANDS, model_width
    )
    inv_rms = lax.rsqrt(jnp.mean(h_rows * h_rows, axis=-1, keepdims=True) + norm_eps)
    unit_rows = h_rows * inv_rms
    scored = unit_rows * out_gain
    query_f = user_query.astype(jnp.float32)
    listwise = jnp.einsum(
        "ucd,ud->uc", scored, query_f, precision=lax.Precision.HIGHEST
    ) / math.sqrt(D)
    top_list = jnp.max(listwise, axis=-1, keepdims=True)
    expo = jnp.exp(listwise - top_list)
    expo_total = jnp.sum(expo, axis=-1, keepdims=True)
    losses = jnp.log(expo_total[:, 0]) + top_list[:, 0] - listwise[:, 0]
    first_one = (jnp.arange(CANDS, dtype=jnp.int32) == 0).astype(jnp.float32)[None, :]
    d_list = loss_scale * (expo / expo_total - first_one)
    d_scored = d_list[..., None] * query_f[:, None, :] / math.sqrt(D)
    d_unit = d_scored * out_gain
    d_h = inv_rms * (d_unit - unit_rows * jnp.mean(d_unit * unit_rows, axis=-1, keepdims=True))
    d_h = d_h.reshape(row_total, model_width)
    d_out = (mix[:, :, None] * d_h[:, None, :]).astype(jnp.bfloat16)
    d_mix = jnp.sum(d_h[:, None, :] * mixed_in.astype(jnp.float32), axis=-1)
    mix_dot = jnp.sum(mix * d_mix, axis=1, keepdims=True)
    d_aff = (d_mix - mix_dot) / aff_total
    d_pick = d_aff * affinity * (1.0 - affinity)
    route_hot = (routes[:, :, None] == jnp.arange(experts, dtype=jnp.int32)).astype(jnp.float32)
    d_logits = jnp.sum(route_hot * d_pick[:, :, None], axis=1).astype(jnp.bfloat16)
    contract_rows = (((0,), (0,)), ((), ()))
    router_term = lax.dot_general(
        normed, d_logits, contract_rows, preferred_element_type=jnp.float32
    )
    grad_send = (
        jnp.zeros((experts * capacity, model_width), jnp.bfloat16)
        .at[slot_dest]
        .set(d_out.reshape(-1, model_width))
    )
    grad_rows = lax.all_to_all(
        grad_send.reshape(experts, capacity, model_width),
        EXPERT,
        split_axis=0,
        concat_axis=0,
        tiled=True,
    ).reshape(slot_count, model_width)
    contract_cols = (((1,), (1,)), ((), ()))
    columns = grad_rows
    d_hidden = lax.dot_general(
        columns, whole_of(w_down[0], DP, 1), contract_cols, preferred_element_type=jnp.float32
    )
    d_gate = (d_hidden * up_pre * silu_grad).astype(jnp.bfloat16)
    d_up = (d_hidden * silu_val).astype(jnp.bfloat16)
    summed = lax.psum_scatter(
        jnp.concatenate(
            [
                lax.dot_general(rows_in, d_gate, contract_rows, preferred_element_type=jnp.float32),
                lax.dot_general(rows_in, d_up, contract_rows, preferred_element_type=jnp.float32),
                lax.dot_general(
                    grad_rows, hidden, contract_rows, preferred_element_type=jnp.float32
                ),
            ],
            axis=1,
        ).astype(jnp.bfloat16),
        DP,
        scatter_dimension=0,
        tiled=True,
    ).astype(jnp.float32)
    grad_gate = summed[:, :FF][None]
    grad_up = summed[:, FF : 2 * FF][None]
    grad_down = summed[:, 2 * FF :].T[None]
    grad_router = over_axes_2(router_term, DP_EXPERT)
    return (losses, grad_gate, grad_up, grad_down, grad_router)


def solution(mesh):
    torus = Mesh(mesh.devices.reshape(8, 2, 4, 4), ("dp_0", "dp_1", "expert_0", "expert_1"))
    return jax.shard_map(
        local,
        mesh=torus,
        in_specs=(
            P(DP_EXPERT, None, None),
            P(DP_EXPERT),
            P(DP_EXPERT, None),
            P(DP_EXPERT, None),
            P(DP_EXPERT, None),
            P(DP_EXPERT, None),
            P(),
            P(EXPERT, DP, None),
            P(EXPERT, DP, None),
            P(EXPERT, None, DP),
            P(),
        ),
        out_specs=(
            P(DP_EXPERT),
            P(EXPERT, DP, None),
            P(EXPERT, DP, None),
            P(EXPERT, None, DP),
            P(),
        ),
        check_vma=False,
    )
```

profile of v0, /device:TPU:2, one launch (start us, length us, event | category | flops | bytes accessed | tf_op | source)
XLA Modules:
  0.0 581.2 jit_solution(2815404170481698003)
XLA Ops:
  8.0 1.8 pad_maximum_fusion.1
  13.2 1.4 scatter_custom_fusion
  15.3 7.5 %all-to-all-start = ((s32[16,1,32]{2,1,0:T(1,128)}), s32[16,1,32]{2,1,0:T(1,128)S(1)}, u32[]{:S(2)}, u32[]{:S(2)}) async-start(s32[16,1,32]{2,1,0:T(1,128)} %all_to_all.18), calls=%async_computation | async-start | bytes 16384 | tf_op jit(solution)/shard_map/all_to_all | solution.py:112
  22.8 3.7 all-gather
  26.6 5.7 fusion.2
  32.5 5.1 fusion.4
  37.9 23.4 %all-gather.3 = f32[16,2,2048]{2,1,0:T(2,128)S(1)} all-gather(f32[1,2,2048]{2,1,0:T(2,128)S(1)} %reshape.537), channel_id=1, replica_groups=mesh['dp_0'=8,'dp_1'=2,'expert_0'=4,'expert_1'=4] {'expert_0','expert_1'}, dimensions={0}, use_global_device_ids=true | all-gather | bytes 278528 | tf_op jit(solution)/shard_map/all_gather | solution.py:116
  61.7 1.4 scatter_custom_fusion.1
  64.2 2.2 mul.310
  66.5 6.3 %all-to-all-start.1 = ((s32[16,1,32]{2,1,0:T(1,128)}), s32[16,1,32]{2,1,0:T(1,128)S(1)}, u32[]{:S(2)}, u32[]{:S(2)}) async-start(s32[16,1,32]{2,1,0:T(1,128)} %all_to_all.20), calls=%async_computation.1 | async-start | bytes 16384 | tf_op jit(solution)/shard_map/all_to_all | solution.py:109
  72.9 5.9 %all-to-all-done.1 = s32[16,1,32]{2,1,0:T(1,128)S(1)} async-done(((s32[16,1,32]{2,1,0:T(1,128)}), s32[16,1,32]{2,1,0:T(1,128)S(1)}, u32[]{:S(2)}, u32[]{:S(2)}) %all-to-all-start.1) | async-done | bytes 2080 | tf_op jit(solution)/shard_map/all_to_all | solution.py:109
  80.2 3.7 gather_fusion.2
  83.8 34.7 %all-gather.12.cloned.1.call-done = bf16[256,2,2048]{2,1,0:T(2,128)(2,1)} async-done(((bf16[1,2,2048]{2,1,0:T(2,128)(2,1)}), bf16[256,2,2048]{2,1,0:T(2,128)(2,1)}) %all-gather.12.cloned.1.call-update) | async-done | bytes 2097168 | tf_op jit(solution)/shard_map/all_gather | solution.py:84
  118.5 2.7 reshape.536
  121.3 3.3 gather_fusion.1
  124.6 3.6 multiply_reduce_fusion
  129.3 2.0 fusion.19
  131.3 34.9 %all-gather.8.cloned.1.call-done = bf16[2048,1536]{1,0:T(8,128)(2,1)} async-done(((bf16[128,1536]{1,0:T(8,128)(2,1)}), bf16[2048,1536]{1,0:T(8,128)(2,1)}) %all-gather.8.cloned.1.call-update) | async-done | bytes 6291472 | tf_op jit(solution)/shard_map/all_gather | solution.py:23
  166.2 4.5 fusion.10
  171.9 3.0 multiply_convert_fusion.4
  174.8 46.7 %all-gather.10.cloned.1.call-done = bf16[1,768,2048]{2,1,0:T(8,128)(2,1)} async-done(((bf16[1,768,256]{2,1,0:T(8,128)(2,1)}), bf16[1,768,2048]{2,1,0:T(8,128)(2,1)}) %all-gather.10.cloned.1.call-update) | async-done | bytes 3145744 | tf_op jit(solution)/shard_map/all_gather | solution.py:30
  221.5 5.1 fusion.16
  226.6 7.7 %all-to-all-start.2 = ((bf16[16,32,2048]{2,1,0:T(8,128)(2,1)}), bf16[16,32,2048]{2,1,0:T(8,128)(2,1)}, u32[]{:S(2)}, u32[]{:S(2)}) async-start(bf16[16,32,2048]{2,1,0:T(8,128)(2,1)} %bitcast.109), calls=%async_computation.2 | async-start | bytes 4194304 | tf_op jit(solution)/shard_map/all_to_all | solution.py:131
  236.6 2.0 gather_fusion.4
  239.3 18.4 %all-to-all-done.2 = bf16[16,32,2048]{2,1,0:T(8,128)(2,1)} async-done(((bf16[16,32,2048]{2,1,0:T(8,128)(2,1)}), bf16[16,32,2048]{2,1,0:T(8,128)(2,1)}, u32[]{:S(2)}, u32[]{:S(2)}) %all-to-all-start.2) | async-done | bytes 2097184 | tf_op jit(solution)/shard_map/all_to_all | solution.py:131
  257.6 4.2 gather_fusion.3
  262.6 2.8 slice_convert_fusion.1
  265.4 3.4 multiply_reduce_fusion.3
  269.0 1.6 copy.111
  270.6 1.7 copy.112
  273.8 2.1 multiply_reduce_fusion.2
  275.9 1.4 subtract_multiply_fusion
  277.7 2.5 mul.322
  280.2 3.8 mul.323
  284.1 4.9 scatter_custom_fusion.2
  288.9 5.9 %all-to-all-start.3 = ((bf16[16,32,2048]{2,1,0:T(8,128)(2,1)}), bf16[16,32,2048]{2,1,0:T(8,128)(2,1)}, u32[]{:S(2)}, u32[]{:S(2)}) async-start(bf16[16,32,2048]{2,1,0:T(8,128)(2,1)} %bitcast.108), calls=%async_computation.3 | async-start | bytes 4194304 | tf_op jit(solution)/shard_map/all_to_all | solution.py:180
  297.1 72.1 %all-reduce.5.cloned.1.call-done = f32[2048,16]{0,1:T(8,128)} async-done(((f32[2048,16]{0,1:T(8,128)}), f32[2048,16]{0,1:T(8,128)}) %all-reduce.5.cloned.1.call-update) | async-done | bytes 131088 | tf_op jit(solution)/shard_map/psum | solution.py:36
  369.3 29.7 %all-reduce.7.cloned.1.call-done = f32[2048,16]{0,1:T(8,128)} async-done(((f32[2048,16]{0,1:T(8,128)}), f32[2048,16]{0,1:T(8,128)}) %all-reduce.7.cloned.1.call-update) | async-done | bytes 131088 | tf_op jit(solution)/shard_map/psum | solution.py:36
  399.1 3.8 convolution_convert_fusion
  402.9 3.6 fusion.12
  406.5 1.9 convolution_convert_fusion.1
  408.4 2.1 convolution_convert_fusion.2
  410.5 4.4 pad_maximum_fusion
  414.9 12.2 %copy.109 = bf16[2048,2304]{1,0:T(8,128)(2,1)} copy(bf16[2048,2304]{0,1:T(8,128)(2,1)} %pad_maximum_fusion) | data formatting | bytes 18874368
  427.8 20.0 %all-reduce.9.cloned.1.call-done = f32[2048,16]{0,1:T(8,128)} async-done(((f32[2048,16]{0,1:T(8,128)}), f32[2048,16]{0,1:T(8,128)}) %all-reduce.9.cloned.1.call-update) | async-done | bytes 131088 | tf_op jit(solution)/shard_map/psum | solution.py:36
  447.8 76.7 %reduce-scatter.4.cloned.1.call-done = bf16[128,2304]{1,0:T(8,128)(2,1)} async-done(((bf16[2048,2304]{1,0:T(8,128)(2,1)}), bf16[128,2304]{1,0:T(8,128)(2,1)}) %reduce-scatter.4.cloned.1.call-update) | async-done | bytes 589840
  528.6 43.9 %all-reduce.11.cloned.1.call-done = f32[2048,16]{0,1:T(8,128)} async-done(((f32[2048,16]{0,1:T(8,128)}), f32[2048,16]{0,1:T(8,128)}) %all-reduce.11.cloned.1.call-update) | async-done | bytes 131088 | tf_op jit(solution)/shard_map/psum | solution.py:36
  572.5 1.6 copy.146
  (157 shorter events, 23.4 us)
Async XLA Ops:
  7.2 229.1 %copy-start = (bf16[2048,16]{0,1:T(8,128)(2,1)S(1)}, bf16[2048,16]{0,1:T(8,128)(2,1)}, u32[]{:S(2)}) copy-start(bf16[2048,16]{0,1:T(8,128)(2,1)} %param.17) | copy-start | bytes 196612
  7.2 19.3 %copy-start.16 = (s32[2]{0:T(128)S(1)}, s32[2]{0:T(128)}, u32[]{:S(2)}) copy-start(s32[2]{0:T(128)} %param.12) | copy-start | bytes 28
  7.2 19.4 %copy-start.11 = (bf16[2,2048]{1,0:T(2,128)(2,1)S(1)}, bf16[2,2048]{1,0:T(2,128)(2,1)}, u32[]{:S(2)}) copy-start(bf16[2,2048]{1,0:T(2,128)(2,1)} %param.13) | copy-start | bytes 24580
  7.2 111.3 %all-gather.12.cloned.1.call-start = ((), (), s32[]{:S(2)}) async-start(), calls=%async_computation.11 | async-start | bytes 2105344 | tf_op jit(solution)/shard_map/all_gather | solution.py:84
  7.9 158.3 %all-gather.8.cloned.1.call-start = ((), (), s32[]{:S(2)}) async-start(), calls=%async_computation.5 | async-start | bytes 6684672 | tf_op jit(solution)/shard_map/all_gather | solution.py:23
  15.3 51.2 %all-to-all-start = ((s32[16,1,32]{2,1,0:T(1,128)}), s32[16,1,32]{2,1,0:T(1,128)S(1)}, u32[]{:S(2)}, u32[]{:S(2)}) async-start(s32[16,1,32]{2,1,0:T(1,128)} %all_to_all.18), calls=%async_computation | async-start | bytes 16384 | tf_op jit(solution)/shard_map/all_to_all | solution.py:112
  22.7 198.8 %all-gather.10.cloned.1.call-start = ((), (), s32[]{:S(2)}) async-start(), calls=%async_computation.10 | async-start | bytes 3538944 | tf_op jit(solution)/shard_map/all_gather | solution.py:30
  32.5 5.1 copy-start.15
  32.5 5.3 copy-start.13
  32.5 31.3 %copy-start.12 = (bf16[2,2048]{1,0:T(2,128)(2,1)S(1)}, bf16[2,2048]{1,0:T(2,128)(2,1)}, u32[]{:S(2)}) copy-start(bf16[2,2048]{1,0:T(2,128)(2,1)} %param.14) | copy-start | bytes 24580
  66.5 12.3 %all-to-all-start.1 = ((s32[16,1,32]{2,1,0:T(1,128)}), s32[16,1,32]{2,1,0:T(1,128)S(1)}, u32[]{:S(2)}, u32[]{:S(2)}) async-start(s32[16,1,32]{2,1,0:T(1,128)} %all_to_all.20), calls=%async_computation.1 | async-start | bytes 16384 | tf_op jit(solution)/shard_map/all_to_all | solution.py:109
  124.6 4.1 copy-start.2
  124.6 4.7 copy-start.3
  166.2 5.6 copy-start.7
  166.2 5.6 copy-start.17
  170.7 1.1 copy-start.19
  174.8 51.7 %copy-start.21 = (bf16[512,768]{1,0:T(8,128)(2,1)}, bf16[512,768]{1,0:T(8,128)(2,1)S(1)}, u32[]{:S(2)}) copy-start(bf16[512,768]{1,0:T(8,128)(2,1)S(1)} %get-tuple-element.59) | copy-start | bytes 2359300
  226.6 7.7 %copy-start.14 = (f32[2048]{0:T(1024)S(1)}, f32[2048]{0:T(1024)}, u32[]{:S(2)}) copy-start(f32[2048]{0:T(1024)} %param.21) | copy-start | bytes 24580
  226.6 31.1 %all-to-all-start.2 = ((bf16[16,32,2048]{2,1,0:T(8,128)(2,1)}), bf16[16,32,2048]{2,1,0:T(8,128)(2,1)}, u32[]{:S(2)}, u32[]{:S(2)}) async-start(bf16[16,32,2048]{2,1,0:T(8,128)(2,1)} %bitcast.109), calls=%async_computation.2 | async-start | bytes 4194304 | tf_op jit(solution)/shard_map/all_to_all | solution.py:131
  235.4 0.8 copy-start.9
  236.3 2.2 copy-start.4
  269.0 3.3 copy-start.10
  270.6 3.2 copy-start.6
  288.9 110.2 %all-to-all-start.3 = ((bf16[16,32,2048]{2,1,0:T(8,128)(2,1)}), bf16[16,32,2048]{2,1,0:T(8,128)(2,1)}, u32[]{:S(2)}, u32[]{:S(2)}) async-start(bf16[16,32,2048]{2,1,0:T(8,128)(2,1)} %bitcast.108), calls=%async_computation.3 | async-start | bytes 4194304 | tf_op jit(solution)/shard_map/all_to_all | solution.py:180
  294.9 1.3 copy-start.5
  294.9 74.4 %all-reduce.5.cloned.1.call-start = ((), (), s32[]{:S(2)}) async-start(), calls=%async_computation.6 | async-start | bytes 262144 | tf_op jit(solution)/shard_map/psum | solution.py:36
  297.1 101.9 %all-reduce.7.cloned.1.call-start = ((), (), s32[]{:S(2)}) async-start(), calls=%async_computation.7 | async-start | bytes 262144 | tf_op jit(solution)/shard_map/psum | solution.py:36
  369.3 78.5 %all-reduce.9.cloned.1.call-start = ((), (), s32[]{:S(2)}) async-start(), calls=%async_computation.8 | async-start | bytes 262144 | tf_op jit(solution)/shard_map/psum | solution.py:36
  399.1 125.4 %reduce-scatter.4.cloned.1.call-start = ((), (), s32[]{:S(2)}) async-start(), calls=%async_computation.12 | async-start | bytes 10027008
  399.1 3.8 copy-start.18
  402.9 3.6 copy-start.8
  402.9 3.6 copy-start.20
  406.5 1.9 copy-start.22
  427.1 145.4 %all-reduce.11.cloned.1.call-start = ((), (), s32[]{:S(2)}) async-start(), calls=%async_computation.9 | async-start | bytes 262144 | tf_op jit(solution)/shard_map/psum | solution.py:36
  525.9 48.2 %copy-start.1 = (bf16[2048,16]{0,1:T(8,128)(2,1)S(1)}, bf16[2048,16]{0,1:T(8,128)(2,1)}, u32[]{:S(2)}) copy-start(bf16[2048,16]{0,1:T(8,128)(2,1)} %param.17) | copy-start | bytes 196612
Sparse Core Ops, SparseCore 0:
  11.8 106.7 all-gather.11
  120.9 45.2 all-gather.7
  168.0 53.5 all-gather.9
  298.3 70.9 all-reduce.4
  371.8 27.1 all-reduce.6
  401.3 46.4 all-reduce.8
  450.3 74.1 reduce-scatter.3
  526.8 45.6 all-reduce.10
where the time goes:
time: 589 us; the launch traced here: 581 us
  waiting for transfers between devices  384 us (65%)
  local copies, waits for them, and re-layouts  59.2 us (10%)
  matrix products  36.6 us (6%)
  other arithmetic  31.9 us (5%)
  starting transfers between devices  27.7 us (5%)
  blocking collectives  27.1 us (5%)
  between operations  15 us (3%)
    psum x4, waiting for transfers between devices, over_axes_2(): x = lax.psum(x, axis)  166 us
    unnamed x9, waiting for transfers between devices  77.5 us
    all_gather x1, waiting for transfers between devices, whole_of(): result = lax.all_gather(result, axes[number], axis=dim, tiled=True)  46.7 us
    all_gather x1, waiting for transfers between devices, sent_together(): result = lax.all_gather(both, axis, axis=dim, tiled=True)  34.9 us
    all_gather x1, waiting for transfers between devices, local(): all_items = lax.all_gather(pos_item, DP_EXPERT, axis=0, tiled=True)  34.7 us
    unnamed x59, local copies, waits for them, and re-layouts  26.9 us
    all_gather x1, blocking collectives, local(): group_ctx = lax.all_gather(context, EXPERT, axis=0, tiled=True)  23.4 us
    all_to_all x1, waiting for transfers between devices, local(): lax.all_to_all(expert_out.reshape(expert_devs, capacity, model_width), EX...  18.4 us
  transfers between devices with their start and end apart: 12, of which 10 were waited for; matrix products, arithmetic and copies ran while one was open for 15% of the time, Pallas kernels for 0%

commit v1 on v0

--- a/solution.py
+++ b/solution.py
@@ -33,7 +33,7 @@
 
 def over_axes_2(x, axes):
     for axis in axes:
-        x = lax.psum(x, axis)
+        x = jnp.sum(lax.all_gather(x, axis), axis=0)
     return x
 
 

time: 589 us -> 439 us (0.75)
  waiting for transfers between devices: 384 us -> 202 us
  blocking collectives: 27.1 us -> 54.7 us
    psum x4 -> x0, waiting for transfers between devices: 166 us -> none  [over_axes_2(): x = lax.psum(x, axis)]
    unnamed x9 -> x6, waiting for transfers between devices: 77.5 us -> 38.8 us
    all_gather x0 -> x3, blocking collectives: none -> 27.7 us  [over_axes_2(): x = jnp.sum(lax.all_gather(x, axis), axis=0)]
    all_to_all x1, waiting for transfers between devices: 0.01 us -> 23 us  [local(): lax.all_to_all(grad_send.reshape(experts, capacity, model_width), EXPERT,...]
  transfers between devices with their start and end apart: 12 -> 9, of which waited for: 10 -> 7; matrix products, arithmetic and copies ran while one was open for 15% -> 20% of each run, Pallas kernels for 0% -> 0%
where the time goes in v1:
time: 439 us; the launch traced here: 431 us
  waiting for transfers between devices  202 us (46%)
  local copies, waits for them, and re-layouts  60.2 us (14%)
  blocking collectives  54.7 us (12%)
  matrix products  37.4 us (9%)
  other arithmetic  33.7 us (8%)
  starting transfers between devices  27.8 us (6%)
  between operations  14.8 us (3%)
    all_gather x1, waiting for transfers between devices, whole_of(): result = lax.all_gather(result, axes[number], axis=dim, tiled=True)  46.7 us
    unnamed x6, waiting for transfers between devices  38.8 us
    all_gather x1, waiting for transfers between devices, sent_together(): result = lax.all_gather(both, axis, axis=dim, tiled=True)  34.9 us
    all_gather x1, waiting for transfers between devices, local(): all_items = lax.all_gather(pos_item, DP_EXPERT, axis=0, tiled=True)  34.7 us
    all_gather x3, blocking collectives, over_axes_2(): x = jnp.sum(lax.all_gather(x, axis), axis=0)  27.7 us
    unnamed x59, local copies, waits for them, and re-layouts  27.2 us
    all_gather x1, blocking collectives, local(): group_ctx = lax.all_gather(context, EXPERT, axis=0, tiled=True)  23.4 us
    all_to_all x1, waiting for transfers between devices, local(): lax.all_to_all(grad_send.reshape(experts, capacity, model_width), EXPERT,...  23 us
  transfers between devices with their start and end apart: 9, of which 7 were waited for; matrix products, arithmetic and copies ran while one was open for 20% of the time, Pallas kernels for 0%

profile of v1, /device:TPU:2, one launch (start us, length us, event | category | flops | bytes accessed | tf_op | source)
XLA Modules:
  0.0 430.9 jit_solution(10429503505124327112)
XLA Ops:
  8.0 1.8 pad_maximum_fusion.1
  13.2 1.4 scatter_custom_fusion
  15.3 7.5 %all-to-all-start = ((s32[16,1,32]{2,1,0:T(1,128)}), s32[16,1,32]{2,1,0:T(1,128)S(1)}, u32[]{:S(2)}, u32[]{:S(2)}) async-start(s32[16,1,32]{2,1,0:T(1,128)} %all_to_all.18), calls=%async_computation | async-start | bytes 16384 | tf_op jit(solution)/shard_map/all_to_all | solution.py:112
  22.8 3.7 all-gather
  26.6 5.7 %fusion.2 = f32[2,16,1,1024]{3,2,1,0:T(1,128)S(1)} fusion(bf16[2,16,128,1]{2,3,1,0:T(2,128)(2,1)S(1)} %reshape.551, bf16[2,1024,2048]{2,1,0:T(8,128)(2,1)} %param.11), kind=kOutput, calls=%fused_computation.11 | convolution fusion | flops 8388608 | bytes 8527872 | tf_op jit(solution)/shard_map/uhd,uthd->uht/dot_general | solution.py:73
  32.5 5.1 %fusion.4 = f32[2,16,1,128]{3,2,1,0:T(1,128)S(1)} fusion(bf16[2,16,1024,1]{2,1,0,3:T(8,128)(2,1)S(1)} %fusion.26, bf16[2,1024,2048]{2,1,0:T(8,128)(2,1)} %param.11), kind=kOutput, calls=%fused_computation.13 | convolution fusion | flops 8388608 | bytes 8470528 | tf_op jit(solution)/shard_map/uht,uthd->uhd/dot_general | solution.py:81
  37.8 23.4 %all-gather.7 = f32[16,2,2048]{2,1,0:T(2,128)S(1)} all-gather(f32[1,2,2048]{2,1,0:T(2,128)S(1)} %reshape.541), channel_id=1, replica_groups=mesh['dp_0'=8,'dp_1'=2,'expert_0'=4,'expert_1'=4] {'expert_0','expert_1'}, dimensions={0}, use_global_device_ids=true | all-gather | bytes 278528 | tf_op jit(solution)/shard_map/all_gather | solution.py:116
  61.7 1.4 scatter_custom_fusion.1
  64.2 2.2 mul.310
  66.5 6.3 %all-to-all-start.1 = ((s32[16,1,32]{2,1,0:T(1,128)}), s32[16,1,32]{2,1,0:T(1,128)S(1)}, u32[]{:S(2)}, u32[]{:S(2)}) async-start(s32[16,1,32]{2,1,0:T(1,128)} %all_to_all.20), calls=%async_computation.1 | async-start | bytes 16384 | tf_op jit(solution)/shard_map/all_to_all | solution.py:109
  72.9 5.9 %all-to-all-done.1 = s32[16,1,32]{2,1,0:T(1,128)S(1)} async-done(((s32[16,1,32]{2,1,0:T(1,128)}), s32[16,1,32]{2,1,0:T(1,128)S(1)}, u32[]{:S(2)}, u32[]{:S(2)}) %all-to-all-start.1) | async-done | bytes 2080 | tf_op jit(solution)/shard_map/all_to_all | solution.py:109
  80.2 3.7 gather_fusion.2
  83.8 34.7 %all-gather.19.cloned.1.call-done = bf16[256,2,2048]{2,1,0:T(2,128)(2,1)} async-done(((bf16[1,2,2048]{2,1,0:T(2,128)(2,1)}), bf16[256,2,2048]{2,1,0:T(2,128)(2,1)}) %all-gather.19.cloned.1.call-update) | async-done | bytes 2097168 | tf_op jit(solution)/shard_map/all_gather | solution.py:84
  118.5 2.7 reshape.540
  121.3 3.3 gather_fusion.1
  124.6 3.6 multiply_reduce_fusion
  129.3 2.0 fusion.19
  131.3 34.9 %all-gather.13.cloned.1.call-done = bf16[2048,1536]{1,0:T(8,128)(2,1)} async-done(((bf16[128,1536]{1,0:T(8,128)(2,1)}), bf16[2048,1536]{1,0:T(8,128)(2,1)}) %all-gather.13.cloned.1.call-update) | async-done | bytes 6291472 | tf_op jit(solution)/shard_map/all_gather | solution.py:23
  166.2 4.5 %fusion.10 = f32[512,768]{1,0:T(8,128)S(1)} fusion(bf16[512,2048]{1,0:T(8,128)(2,1)} %fusion.19, bf16[2048,1536]{1,0:T(8,128)(2,1)} %all-gather.13.cloned.1.call-done), kind=kOutput, calls=%fused_computation.25 | convolution fusion | flops 1610612736 | bytes 6815744 | tf_op jit(solution)/shard_map/dot_general | solution.py:124
  171.9 3.0 multiply_convert_fusion.4
  174.8 46.7 %all-gather.15.cloned.1.call-done = bf16[1,768,2048]{2,1,0:T(8,128)(2,1)} async-done(((bf16[1,768,256]{2,1,0:T(8,128)(2,1)}), bf16[1,768,2048]{2,1,0:T(8,128)(2,1)}) %all-gather.15.cloned.1.call-update) | async-done | bytes 3145744 | tf_op jit(solution)/shard_map/all_gather | solution.py:30
  221.5 5.1 %fusion.16 = bf16[512,2048]{1,0:T(8,128)(2,1)} fusion(bf16[512,768]{1,0:T(8,128)(2,1)S(1)} %get-tuple-element.69, bf16[1,768,2048]{2,1,0:T(8,128)(2,1)} %all-gather.15.cloned.1.call-done), kind=kOutput, calls=%fused_computation.31 | convolution fusion | flops 1611661312 | bytes 6029312 | tf_op jit(solution)/shard_map/dot_general | solution.py:128
  226.6 7.7 %all-to-all-start.2 = ((bf16[16,32,2048]{2,1,0:T(8,128)(2,1)}), bf16[16,32,2048]{2,1,0:T(8,128)(2,1)}, u32[]{:S(2)}, u32[]{:S(2)}) async-start(bf16[16,32,2048]{2,1,0:T(8,128)(2,1)} %bitcast.120), calls=%async_computation.2 | async-start | bytes 4194304 | tf_op jit(solution)/shard_map/all_to_all | solution.py:131
  236.6 2.0 gather_fusion.4
  239.3 18.3 %all-to-all-done.2 = bf16[16,32,2048]{2,1,0:T(8,128)(2,1)} async-done(((bf16[16,32,2048]{2,1,0:T(8,128)(2,1)}), bf16[16,32,2048]{2,1,0:T(8,128)(2,1)}, u32[]{:S(2)}, u32[]{:S(2)}) %all-to-all-start.2) | async-done | bytes 2097184 | tf_op jit(solution)/shard_map/all_to_all | solution.py:131
  257.6 4.2 gather_fusion.3
  262.6 2.8 slice_convert_fusion.1
  265.4 3.4 multiply_reduce_fusion.3
  269.0 1.6 copy.139
  270.6 1.7 copy.140
  273.8 2.1 multiply_reduce_fusion.2
  275.9 1.4 subtract_multiply_fusion
  277.7 2.5 mul.322
  280.2 3.7 mul.323
  283.9 4.9 %scatter_custom_fusion.2 = bf16[512,2048]{1,0:T(8,128)(2,1)} fusion(s32[256]{0:T(256)S(1)} %bitcast.137, f32[256,2048]{1,0:T(8,128)} %mul.323, f32[256]{0:T(256)S(1)} %mul.302, bf16[]{:T(256)} %constant.92.clone.1), kind=kCustom, calls=%fused_computation.46 | custom fusion | flops 1048576 | bytes 4195330 | tf_op jit(solution)/shard_map/scatter | solution.py:178
  288.8 5.9 %all-to-all-start.3 = ((bf16[16,32,2048]{2,1,0:T(8,128)(2,1)}), bf16[16,32,2048]{2,1,0:T(8,128)(2,1)}, u32[]{:S(2)}, u32[]{:S(2)}) async-start(bf16[16,32,2048]{2,1,0:T(8,128)(2,1)} %bitcast.119), calls=%async_computation.3 | async-start | bytes 4194304 | tf_op jit(solution)/shard_map/all_to_all | solution.py:180
  297.2 23.0 %all-to-all-done.3 = bf16[16,32,2048]{2,1,0:T(8,128)(2,1)} async-done(((bf16[16,32,2048]{2,1,0:T(8,128)(2,1)}), bf16[16,32,2048]{2,1,0:T(8,128)(2,1)}, u32[]{:S(2)}, u32[]{:S(2)}) %all-to-all-start.3) | async-done | bytes 2097184 | tf_op jit(solution)/shard_map/all_to_all | solution.py:180
  320.1 4.5 %fusion.12 = f32[512,768]{1,0:T(8,128)S(1)} fusion(bf16[512,2048]{1,0:T(8,128)(2,1)} %bitcast.24, bf16[1,768,2048]{2,1,0:T(8,128)(2,1)} %all-gather.15.cloned.1.call-done), kind=kOutput, calls=%fused_computation.27 | convolution fusion | flops 1610612736 | bytes 6815744 | tf_op jit(solution)/shard_map/dot_general | solution.py:189
  324.7 1.9 convolution_convert_fusion.1
  326.6 3.6 convolution_convert_fusion
  330.2 2.1 convolution_convert_fusion.2
  332.3 4.4 %pad_maximum_fusion = bf16[2048,2304]{0,1:T(8,128)(2,1)} fusion(bf16[2048,768]{0,1:T(8,128)(2,1)S(1)} %convolution_convert_fusion, bf16[2048,768]{0,1:T(8,128)(2,1)S(1)} %convolution_convert_fusion.1, bf16[2048,768]{0,1:T(8,128)(2,1)S(1)} %convolution_convert_fusion.2), kind=kLoop, calls=%fused_computation.10 | loop fusion | flops 28311552 | bytes 18874368 | tf_op jit(solution)/shard_map/concatenate | solution.py:195
  336.7 12.2 %copy.137 = bf16[2048,2304]{1,0:T(8,128)(2,1)} copy(bf16[2048,2304]{0,1:T(8,128)(2,1)} %pad_maximum_fusion) | data formatting | bytes 18874368
  349.5 1.8 copy.145
  351.6 2.0 all-gather.3
  354.2 12.9 %all-gather.4 = f32[8192,16]{0,1:T(8,128)S(1)} all-gather(f32[2048,16]{0,1:T(8,128)S(1)} %reduce_sum.147), channel_id=6, replica_groups=mesh['dp_0'=8,'dp_1'=2,'expert_0'=4,'expert_1'=4] {'expert_0'}, dimensions={0}, use_global_device_ids=true | all-gather | bytes 655360 | tf_op jit(solution)/shard_map/all_gather | solution.py:36
  367.7 12.8 %all-gather.5 = f32[8192,16]{0,1:T(8,128)S(1)} all-gather(f32[2048,16]{0,1:T(8,128)S(1)} %reduce_sum.148), channel_id=7, replica_groups=mesh['dp_0'=8,'dp_1'=2,'expert_0'=4,'expert_1'=4] {'expert_1'}, dimensions={0}, use_global_device_ids=true | all-gather | bytes 655360 | tf_op jit(solution)/shard_map/all_gather | solution.py:36
  381.8 38.1 %reduce-scatter.4.cloned.1.call-done = bf16[128,2304]{1,0:T(8,128)(2,1)} async-done(((bf16[2048,2304]{1,0:T(8,128)(2,1)}), bf16[128,2304]{1,0:T(8,128)(2,1)}) %reduce-scatter.4.cloned.1.call-update) | async-done | bytes 589840
  (158 shorter events, 26.2 us)
Async XLA Ops:
  7.2 229.2 %copy-start = (bf16[2048,16]{0,1:T(8,128)(2,1)S(1)}, bf16[2048,16]{0,1:T(8,128)(2,1)}, u32[]{:S(2)}) copy-start(bf16[2048,16]{0,1:T(8,128)(2,1)} %param.17) | copy-start | bytes 196612
  7.2 19.3 %copy-start.16 = (s32[2]{0:T(128)S(1)}, s32[2]{0:T(128)}, u32[]{:S(2)}) copy-start(s32[2]{0:T(128)} %param.12) | copy-start | bytes 28
  7.2 19.4 %copy-start.11 = (bf16[2,2048]{1,0:T(2,128)(2,1)S(1)}, bf16[2,2048]{1,0:T(2,128)(2,1)}, u32[]{:S(2)}) copy-start(bf16[2,2048]{1,0:T(2,128)(2,1)} %param.13) | copy-start | bytes 24580
  7.2 111.3 %all-gather.19.cloned.1.call-start = ((), (), s32[]{:S(2)}) async-start(), calls=%async_computation.8 | async-start | bytes 2105344 | tf_op jit(solution)/shard_map/all_gather | solution.py:84
  7.9 158.3 %all-gather.13.cloned.1.call-start = ((), (), s32[]{:S(2)}) async-start(), calls=%async_computation.5 | async-start | bytes 6684672 | tf_op jit(solution)/shard_map/all_gather | solution.py:23
  15.3 51.2 %all-to-all-start = ((s32[16,1,32]{2,1,0:T(1,128)}), s32[16,1,32]{2,1,0:T(1,128)S(1)}, u32[]{:S(2)}, u32[]{:S(2)}) async-start(s32[16,1,32]{2,1,0:T(1,128)} %all_to_all.18), calls=%async_computation | async-start | bytes 16384 | tf_op jit(solution)/shard_map/all_to_all | solution.py:112
  22.7 198.8 %all-gather.15.cloned.1.call-start = ((), (), s32[]{:S(2)}) async-start(), calls=%async_computation.6 | async-start | bytes 3538944 | tf_op jit(solution)/shard_map/all_gather | solution.py:30
  32.5 5.1 %copy-start.15 = (s32[2,63]{1,0:T(2,128)S(1)}, s32[2,63]{1,0:T(2,128)}, u32[]{:S(2)}) copy-start(s32[2,63]{1,0:T(2,128)} %param.15) | copy-start | bytes 1516
  32.5 5.3 %copy-start.13 = (s32[128,2]{0,1:T(2,128)S(1)}, s32[128,2]{0,1:T(2,128)}, u32[]{:S(2)}) copy-start(s32[128,2]{0,1:T(2,128)} %param.16) | copy-start | bytes 3076
  32.5 31.3 %copy-start.12 = (bf16[2,2048]{1,0:T(2,128)(2,1)S(1)}, bf16[2,2048]{1,0:T(2,128)(2,1)}, u32[]{:S(2)}) copy-start(bf16[2,2048]{1,0:T(2,128)(2,1)} %param.14) | copy-start | bytes 24580
  66.5 12.3 %all-to-all-start.1 = ((s32[16,1,32]{2,1,0:T(1,128)}), s32[16,1,32]{2,1,0:T(1,128)S(1)}, u32[]{:S(2)}, u32[]{:S(2)}) async-start(s32[16,1,32]{2,1,0:T(1,128)} %all_to_all.20), calls=%async_computation.1 | async-start | bytes 16384 | tf_op jit(solution)/shard_map/all_to_all | solution.py:109
  124.6 4.1 copy-start.2
  124.6 4.7 %copy-start.3 = (bf16[512,2048]{1,0:T(8,128)(2,1)S(1)}, bf16[512,2048]{1,0:T(8,128)(2,1)}, u32[]{:S(2)}) copy-start(bf16[512,2048]{1,0:T(8,128)(2,1)} %gather_fusion.1) | copy-start | bytes 6291460
  166.2 5.6 %copy-start.7 = (bf16[512,2048]{1,0:T(8,128)(2,1)S(1)}, bf16[512,2048]{1,0:T(8,128)(2,1)}, u32[]{:S(2)}) copy-start(bf16[512,2048]{1,0:T(8,128)(2,1)} %fusion.19) | copy-start | bytes 6291460
  166.2 5.6 %copy-start.17 = (bf16[2048,1536]{1,0:T(8,128)(2,1)S(1)}, bf16[2048,1536]{1,0:T(8,128)(2,1)}, u32[]{:S(2)}) copy-start(bf16[2048,1536]{1,0:T(8,128)(2,1)} %all-gather.13.cloned.1.call-done) | copy-start | bytes 18874372
  170.7 1.1 copy-start.18
  174.8 51.7 %copy-start.20 = (bf16[512,768]{1,0:T(8,128)(2,1)}, bf16[512,768]{1,0:T(8,128)(2,1)S(1)}, u32[]{:S(2)}) copy-start(bf16[512,768]{1,0:T(8,128)(2,1)S(1)} %get-tuple-element.69) | copy-start | bytes 2359300
  226.6 7.7 %copy-start.14 = (f32[2048]{0:T(1024)S(1)}, f32[2048]{0:T(1024)}, u32[]{:S(2)}) copy-start(f32[2048]{0:T(1024)} %param.21) | copy-start | bytes 24580
  226.6 31.1 %all-to-all-start.2 = ((bf16[16,32,2048]{2,1,0:T(8,128)(2,1)}), bf16[16,32,2048]{2,1,0:T(8,128)(2,1)}, u32[]{:S(2)}, u32[]{:S(2)}) async-start(bf16[16,32,2048]{2,1,0:T(8,128)(2,1)} %bitcast.120), calls=%async_computation.2 | async-start | bytes 4194304 | tf_op jit(solution)/shard_map/all_to_all | solution.py:131
  235.4 0.8 copy-start.9
  236.3 2.2 copy-start.4
  269.0 3.3 copy-start.10
  270.6 3.2 copy-start.6
  288.8 31.4 %all-to-all-start.3 = ((bf16[16,32,2048]{2,1,0:T(8,128)(2,1)}), bf16[16,32,2048]{2,1,0:T(8,128)(2,1)}, u32[]{:S(2)}, u32[]{:S(2)}) async-start(bf16[16,32,2048]{2,1,0:T(8,128)(2,1)} %bitcast.119), calls=%async_computation.3 | async-start | bytes 4194304 | tf_op jit(solution)/shard_map/all_to_all | solution.py:180
  294.7 1.3 copy-start.5
  294.7 54.8 %all-gather.17.cloned.1.call-start = ((), (), s32[]{:S(2)}) async-start(), calls=%async_computation.7 | async-start | bytes 1179648 | tf_op jit(solution)/shard_map/all_gather | solution.py:36
  296.9 123.0 %reduce-scatter.4.cloned.1.call-start = ((), (), s32[]{:S(2)}) async-start(), calls=%async_computation.9 | async-start | bytes 10027008
  320.1 4.5 %copy-start.8 = (bf16[512,2048]{1,0:T(8,128)(2,1)S(1)}, bf16[512,2048]{1,0:T(8,128)(2,1)}, u32[]{:S(2)}) copy-start(bf16[512,2048]{1,0:T(8,128)(2,1)} %fusion.19) | copy-start | bytes 6291460
  320.1 4.6 %copy-start.19 = (f32[512,768]{1,0:T(8,128)S(1)}, f32[512,768]{1,0:T(8,128)}, u32[]{:S(2)}) copy-start(f32[512,768]{1,0:T(8,128)} %copy-done.18) | copy-start | bytes 4718596
  324.7 1.9 copy-start.21
  326.6 3.6 copy-start.22
  421.3 2.8 copy-start.1
Sparse Core Ops, SparseCore 0:
  11.8 106.7 all-gather.18
  120.9 45.2 all-gather.12
  168.0 53.5 all-gather.14
  297.6 37.7 all-gather.16
  349.0 70.8 reduce-scatter.3
